TPU v7x, 32 devices: a whole 2x2x4 slice. The times are simulated.
32 devices in a mesh: group: 2 (over y), expert: 4 (over z), dp: 4 (over x, core).
Axes of the slice: x: 2, y: 2, z: 4, core: 2. Of those that a mesh axis runs over, the one named last changes fastest.
Arguments:
- latent_in: bfloat16 [2048, 1024], P(('group', 'expert', 'dp')), parts along dimension 0, may hold values from -6 to 6
- routes: int32 [2048, 8], P(('group', 'expert', 'dp')), parts along dimension 0, may hold values from 0 to 15, all different within a row; in each aligned block of 64 rows (0 to 63, 64 to 127, ...) at most 36 rows name the same one
- gates: float32 [2048, 8], P(('group', 'expert', 'dp')), parts along dimension 0, may hold values from 0.02 to 0.3
- up_weight: bfloat16 [16, 1024, 1024], P('expert', 'dp'), may hold values from -0.1875 to 0.1875
- down_weight: bfloat16 [16, 1024, 1024], P('expert', 'dp'), may hold values from -0.1875 to 0.1875
- out_grad: bfloat16 [2048, 1024], P(('group', 'expert', 'dp')), parts along dimension 0, may hold values from -6 to 6
Outputs:
- latent_out: bfloat16 [2048, 1024], P(('group', 'expert', 'dp')), parts along dimension 0
- grad_in: bfloat16 [2048, 1024], P(('group', 'expert', 'dp')), parts along dimension 0
- gate_grad: float32 [2048, 8], P(('group', 'expert', 'dp')), parts along dimension 0
- grad_up: float32 [32, 1024, 1024], P(('group', 'expert'), 'dp'), parts along dimension 0
- grad_down: float32 [32, 1024, 1024], P(('group', 'expert'), 'dp'), parts along dimension 0
There are 2 independent parts, one for each index of `group`. A program takes and returns all parts, laid end to end along the dimension named above; an argument that names none is the same for every part. Nothing has to cross between parts.
Inputs may be any that keep to these rules, and one draw needn't show every extreme that they name: `routes`: in each aligned block of 64 rows (the rows of one device) no expert is named by more than 36 rows, and in some blocks one is named by exactly 36; the 8 experts of a row differ.
All inputs are finite; a program needn't handle non-finite values.
Results may differ from a plain program's by a relative error of at most 0.015.
Values may be sent and summed in bfloat16 or wider, within the bound.
A program may use at most 128 MiB of HBM per device.

v0:
```python
import jax
import jax.numpy as jnp
from jax import lax
from jax.sharding import PartitionSpec as P


def slot_places(routes, expert_total, capacity):
    flat_ids = routes.reshape(-1)
    pair_count = flat_ids.shape[0]
    onehot = (flat_ids[:, None] == jnp.arange(expert_total, dtype=jnp.int32)[None, :]).astype(
        jnp.int32
    )
    earlier = jnp.cumsum(onehot, axis=0) - onehot
    slot_ids = jnp.sum(earlier * onehot, axis=1)
    places = flat_ids * capacity + slot_ids
    empty = jnp.full((expert_total * capacity,), pair_count, jnp.int32)
    pair_of = empty.at[places].set(jnp.arange(pair_count, dtype=jnp.int32))
    return (places, pair_of)


def local(latent_in, routes, gates, up_weight, down_weight, out_grad):
    owner_count = lax.axis_size("expert")
    local_experts = up_weight.shape[0]
    expert_total = local_experts * owner_count
    token_rows, route_count = routes.shape
    latent = latent_in.shape[1]
    capacity = 9 * token_rows * route_count // (8 * expert_total)
    places, pair_of = slot_places(routes, expert_total, capacity)
    token_of = pair_of // route_count
    zero_row = jnp.zeros((1, latent), jnp.bfloat16)
    padded_in = jnp.concatenate([latent_in, zero_row], axis=0)
    padded_grad = jnp.concatenate([out_grad, zero_row], axis=0)
    padded_gates = jnp.concatenate([gates.reshape(-1), jnp.zeros((1,), jnp.float32)])
    slot_gates = padded_gates[pair_of]
    send_shape = (owner_count, local_experts * capacity, latent)
    block_shape = (owner_count, local_experts, capacity, latent)
    send_rows = padded_in[token_of].reshape(send_shape)
    send_grad = (
        (slot_gates[:, None] * padded_grad[token_of].astype(jnp.float32))
        .astype(jnp.bfloat16)
        .reshape(send_shape)
    )
    up_full, down_full = (
        lax.all_gather(up_weight, "dp", axis=1, tiled=True),
        lax.all_gather(down_weight, "dp", axis=1, tiled=True),
    )
    arrived = lax.all_to_all(send_rows, "expert", split_axis=0, concat_axis=0, tiled=True)
    forward_rows_four = arrived.reshape(block_shape)
    pre_act = jnp.einsum(
        "secl,elh->sech", forward_rows_four, up_full, preferred_element_type=jnp.float32
    )
    active = jnp.maximum(pre_act, 0.0)
    forward_hidden = (active * active).astype(jnp.bfloat16)
    result = jnp.einsum(
        "sech,ehl->secl", forward_hidden, down_full, preferred_element_type=jnp.float32
    ).astype(jnp.bfloat16)
    rows_four, active, hidden, result = (
        forward_rows_four,
        active,
        forward_hidden,
        result.reshape(send_shape),
    )
    returned = lax.all_to_all(result, "expert", split_axis=0, concat_axis=0, tiled=True)
    arrived_grad = lax.all_to_all(send_grad, "expert", split_axis=0, concat_axis=0, tiled=True)
    backward_grad_four = arrived_grad.reshape(block_shape)
    hidden_grad = jnp.einsum(
        "secl,ehl->sech", backward_grad_four, down_full, preferred_element_type=jnp.float32
    )
    backward_pre_grad = (hidden_grad * 2.0 * active).astype(jnp.bfloat16)
    row_grad = jnp.einsum(
        "sech,elh->secl", backward_pre_grad, up_full, preferred_element_type=jnp.float32
    ).astype(jnp.bfloat16)
    grad_four, pre_grad, row_grad = (
        backward_grad_four,
        backward_pre_grad,
        row_grad.reshape(send_shape),
    )
    returned_grad = lax.all_to_all(row_grad, "expert", split_axis=0, concat_axis=0, tiled=True)
    picked = (
        returned.reshape(expert_total * capacity, latent)[places]
        .reshape(token_rows, route_count, latent)
        .astype(jnp.float32)
    )
    latent_out = jnp.sum(gates[:, :, None] * picked, axis=1).astype(jnp.bfloat16)
    gate_grad = jnp.sum(out_grad.astype(jnp.float32)[:, None, :] * picked, axis=2)
    picked_grad = (
        returned_grad.reshape(expert_total * capacity, latent)[places]
        .reshape(token_rows, route_count, latent)
        .astype(jnp.float32)
    )
    grad_in = jnp.sum(picked_grad, axis=1).astype(jnp.bfloat16)
    up_sum = lax.psum_scatter(
        jnp.einsum(
            "secl,sech->leh", rows_four, pre_grad, preferred_element_type=jnp.float32
        ).astype(jnp.bfloat16),
        "dp",
        scatter_dimension=0,
        tiled=True,
    ).astype(jnp.float32)
    down_sum = lax.psum_scatter(
        jnp.einsum("sech,secl->hel", hidden, grad_four, preferred_element_type=jnp.float32).astype(
            jnp.bfloat16
        ),
        "dp",
        scatter_dimension=0,
        tiled=True,
    ).astype(jnp.float32)
    grad_up = jnp.transpose(up_sum, (1, 0, 2))
    grad_down = jnp.transpose(down_sum, (1, 0, 2))
    return (latent_out, grad_in, gate_grad, grad_up, grad_down)


def solution(mesh):
    in_specs = (
        P(("group", "expert", "dp"), None),
        P(("group", "expert", "dp"), None),
        P(("group", "expert", "dp"), None),
        P("expert", "dp", None),
        P("expert", "dp", None),
        P(("group", "expert", "dp"), None),
    )
    out_specs = (
        P(("group", "expert", "dp"), None),
        P(("group", "expert", "dp"), None),
        P(("group", "expert", "dp"), None),
        P(("group", "expert"), "dp", None),
        P(("group", "expert"), "dp", None),
    )
    return jax.shard_map(local, mesh=mesh, in_specs=in_specs, out_specs=out_specs, check_vma=False)
```

profile of v0, /device:TPU:0, one launch (start us, length us, event | category | flops | bytes accessed | tf_op | source)
XLA Modules:
  0.0 306.2 jit_solution(17737343662307431461)
XLA Ops:
  13.2 3.4 %gather_fusion = bf16[576,1024]{1,0:T(8,128)(2,1)} fusion(bf16[65,1024]{1,0:T(8,128)(2,1)S(1)} %concatenate.9, s32[1024]{0:T(1024)S(1)} %get-tuple-element.30), kind=kCustom, calls=%fused_computation | custom fusion | bytes 2361600 | tf_op jit(solution)/shard_map/gather | solution.py:37
  16.6 6.4 %all-to-all-start = ((bf16[4,144,1024]{2,1,0:T(8,128)(2,1)}), bf16[4,144,1024]{2,1,0:T(8,128)(2,1)S(1)}, u32[]{:S(2)}, u32[]{:S(2)}) async-start(bf16[4,144,1024]{2,1,0:T(8,128)(2,1)} %bitcast.3), calls=%async_computation | async-start | bytes 2359296 | tf_op jit(solution)/shard_map/all_to_all | solution.py:47
  23.2 2.9 gather_fusion.3
  26.1 2.6 gather_fusion.2
  30.1 21.5 %all-to-all-done = bf16[4,144,1024]{2,1,0:T(8,128)(2,1)S(1)} async-done(((bf16[4,144,1024]{2,1,0:T(8,128)(2,1)}), bf16[4,144,1024]{2,1,0:T(8,128)(2,1)S(1)}, u32[]{:S(2)}, u32[]{:S(2)}) %all-to-all-start) | async-done | bytes 1179680 | tf_op jit(solution)/shard_map/all_to_all | solution.py:47
  51.6 3.5 %all-to-all-start.2 = ((bf16[4,144,1024]{2,1,0:T(8,128)(2,1)}), bf16[4,144,1024]{2,1,0:T(8,128)(2,1)S(1)}, u32[]{:S(2)}, u32[]{:S(2)}) async-start(bf16[4,144,1024]{2,1,0:T(8,128)(2,1)} %fusion.10), calls=%async_computation.2 | async-start | bytes 2359296 | tf_op jit(solution)/shard_map/all_to_all | solution.py:64
  57.3 25.8 %all-to-all-done.2 = bf16[4,144,1024]{2,1,0:T(8,128)(2,1)S(1)} async-done(((bf16[4,144,1024]{2,1,0:T(8,128)(2,1)}), bf16[4,144,1024]{2,1,0:T(8,128)(2,1)S(1)}, u32[]{:S(2)}, u32[]{:S(2)}) %all-to-all-start.2) | async-done | bytes 1179680 | tf_op jit(solution)/shard_map/all_to_all | solution.py:64
  85.1 5.5 %fusion.2 = f32[4,4,36,1024]{3,2,1,0:T(8,128)S(1)} fusion(bf16[4,1024,1024]{2,1,0:T(8,128)(2,1)} %all-gather.3.cloned.1.call-done, bf16[4,4,36,1024]{3,0,2,1:T(4,128)(2,1)} %bitcast.94), kind=kOutput, calls=%fused_computation.10 | convolution fusion | flops 1207959552 | bytes 11927552 | tf_op jit(solution)/shard_map/secl,elh->sech/dot_general | solution.py:49
  90.6 39.9 %all-gather.5.cloned.1.call-done = bf16[4,1024,1024]{2,1,0:T(8,128)(2,1)} async-done(((bf16[4,256,1024]{2,1,0:T(8,128)(2,1)}), bf16[4,1024,1024]{2,1,0:T(8,128)(2,1)}) %all-gather.5.cloned.1.call-update) | async-done | bytes 8388624 | tf_op jit(solution)/shard_map/all_gather | solution.py:45
  130.5 6.8 %fusion.27 = bf16[4,4,36,1024]{3,2,0,1:T(8,128)(2,1)S(1)} fusion(f32[4,4,36,1024]{3,2,1,0:T(8,128)S(1)} %fusion.2, bf16[4,1024,1024]{2,1,0:T(8,128)(2,1)} %all-gather.5.cloned.1.call-done, bf16[4,4,36,1024]{3,0,2,1:T(4,128)(2,1)} %bitcast.96), kind=kOutput, calls=%fused_computation.32 | convolution fusion | flops 1210318848 | bytes 13107200 | tf_op jit(solution)/shard_map/secl,ehl->sech/dot_general | solution.py:66
  138.4 5.8 %fusion.8 = bf16[1024,4,1024]{0,2,1:T(8,128)(2,1)} fusion(bf16[4,4,36,1024]{3,2,0,1:T(8,128)(2,1)S(1)} %fusion.27, bf16[4,4,36,1024]{3,0,2,1:T(4,128)(2,1)S(1)} %bitcast.95), kind=kOutput, calls=%fused_computation.16 | convolution fusion | flops 1212153856 | bytes 10747904 | tf_op jit(solution)/shard_map/secl,sech->leh/dot_general | solution.py:93
  144.4 7.8 %fusion.9 = bf16[1024,4,1024]{0,2,1:T(8,128)(2,1)} fusion(bf16[4,4,36,1024]{3,0,2,1:T(4,128)(2,1)} %bitcast.97, f32[4,4,36,1024]{3,2,1,0:T(8,128)S(1)} %fusion.2), kind=kOutput, calls=%fused_computation.17 | convolution fusion | flops 1213923328 | bytes 11927552 | tf_op jit(solution)/shard_map/sech,secl->hel/dot_general | solution.py:101
  152.3 6.8 %fusion.24 = bf16[4,4,36,1024]{3,2,0,1:T(8,128)(2,1)S(1)} fusion(bf16[4,1024,1024]{2,1,0:T(8,128)(2,1)} %all-gather.5.cloned.1.call-done, f32[4,4,36,1024]{3,2,1,0:T(8,128)S(1)} %fusion.2), kind=kOutput, calls=%fused_computation.31 | convolution fusion | flops 1210318848 | bytes 11927552 | tf_op jit(solution)/shard_map/sech,ehl->secl/dot_general | solution.py:54
  161.4 4.4 %all-to-all-start.1 = ((bf16[4,144,1024]{2,1,0:T(8,128)(2,1)}), bf16[4,144,1024]{2,1,0:T(8,128)(2,1)S(1)}, u32[]{:S(2)}, u32[]{:S(2)}) async-start(bf16[4,144,1024]{2,1,0:T(8,128)(2,1)} %copy.59), calls=%async_computation.1 | async-start | bytes 2359296 | tf_op jit(solution)/shard_map/all_to_all | solution.py:63
  165.7 6.9 %fusion.21 = bf16[4,4,36,1024]{3,2,0,1:T(8,128)(2,1)S(1)} fusion(bf16[4,4,36,1024]{3,2,0,1:T(8,128)(2,1)S(1)} %copy-done.2, bf16[4,1024,1024]{2,1,0:T(8,128)(2,1)} %all-gather.3.cloned.1.call-done), kind=kOutput, calls=%fused_computation.30 | convolution fusion | flops 1208549376 | bytes 10747904 | tf_op jit(solution)/shard_map/sech,elh->secl/dot_general | solution.py:70
  175.0 19.7 %all-to-all-done.1 = bf16[4,144,1024]{2,1,0:T(8,128)(2,1)S(1)} async-done(((bf16[4,144,1024]{2,1,0:T(8,128)(2,1)}), bf16[4,144,1024]{2,1,0:T(8,128)(2,1)S(1)}, u32[]{:S(2)}, u32[]{:S(2)}) %all-to-all-start.1) | async-done | bytes 1179680 | tf_op jit(solution)/shard_map/all_to_all | solution.py:63
  194.7 3.8 %all-to-all-start.3 = ((bf16[4,144,1024]{2,1,0:T(8,128)(2,1)}), bf16[4,144,1024]{2,1,0:T(8,128)(2,1)S(1)}, u32[]{:S(2)}, u32[]{:S(2)}) async-start(bf16[4,144,1024]{2,1,0:T(8,128)(2,1)} %copy.64), calls=%async_computation.3 | async-start | bytes 2359296 | tf_op jit(solution)/shard_map/all_to_all | solution.py:78
  201.3 25.0 %all-to-all-done.3 = bf16[4,144,1024]{2,1,0:T(8,128)(2,1)S(1)} async-done(((bf16[4,144,1024]{2,1,0:T(8,128)(2,1)}), bf16[4,144,1024]{2,1,0:T(8,128)(2,1)S(1)}, u32[]{:S(2)}, u32[]{:S(2)}) %all-to-all-start.3) | async-done | bytes 1179680 | tf_op jit(solution)/shard_map/all_to_all | solution.py:78
  228.3 2.6 fusion.12
  232.9 4.1 %convert_bitcast_fusion.1 = f32[4,256,1024]{1,2,0:T(8,128)} fusion(bf16[256,4,1024]{0,2,1:T(8,128)(2,1)} %reduce-scatter.3.cloned.1.call-done), kind=kLoop, calls=%fused_computation.19 | loop fusion | flops 1048576 | bytes 6291456 | tf_op jit(solution)/shard_map/transpose | solution.py:108
  237.0 5.3 %copy.68 = f32[4,256,1024]{2,1,0:T(8,128)} copy(f32[4,256,1024]{1,2,0:T(8,128)} %convert_bitcast_fusion.1) | data formatting | bytes 8388608
  242.4 48.1 %reduce-scatter.5.cloned.1.call-done = bf16[256,4,1024]{0,2,1:T(8,128)(2,1)} async-done(((bf16[1024,4,1024]{0,2,1:T(8,128)(2,1)}), bf16[256,4,1024]{0,2,1:T(8,128)(2,1)}) %reduce-scatter.5.cloned.1.call-update) | async-done | bytes 2097168 | tf_op jit(solution)/shard_map/reduce_scatter | solution.py:100
  290.4 3.9 %convert_bitcast_fusion = f32[4,256,1024]{1,2,0:T(8,128)} fusion(bf16[256,4,1024]{0,2,1:T(8,128)(2,1)} %reduce-scatter.5.cloned.1.call-done), kind=kLoop, calls=%fused_computation.18 | loop fusion | flops 1048576 | bytes 6291456 | tf_op jit(solution)/shard_map/transpose | solution.py:109
  294.3 5.3 %copy.69 = f32[4,256,1024]{2,1,0:T(8,128)} copy(f32[4,256,1024]{1,2,0:T(8,128)} %convert_bitcast_fusion) | data formatting | bytes 8388608
  (60 shorter events, 24.3 us)
Async XLA Ops:
  7.2 1.5 copy-start.5
  7.2 3.4 %copy-start.4 = (bf16[64,1024]{1,0:T(8,128)(2,1)S(1)}, bf16[64,1024]{1,0:T(8,128)(2,1)}, u32[]{:S(2)}) copy-start(bf16[64,1024]{1,0:T(8,128)(2,1)} %param.6) | copy-start | bytes 393220
  7.2 77.9 %all-gather.3.cloned.1.call-start = ((), (), s32[]{:S(2)}) async-start(), calls=%async_computation.6 | async-start | bytes 10485760 | tf_op jit(solution)/shard_map/all_gather | solution.py:44
  7.9 122.6 %all-gather.5.cloned.1.call-start = ((), (), s32[]{:S(2)}) async-start(), calls=%async_computation.7 | async-start | bytes 10485760 | tf_op jit(solution)/shard_map/all_gather | solution.py:45
  16.6 6.5 %copy-start.6 = (f32[64,8]{0,1:T(8,128)S(1)}, f32[64,8]{0,1:T(8,128)}, u32[]{:S(2)}) copy-start(f32[64,8]{0,1:T(8,128)} %param.8) | copy-start | bytes 6148
  16.6 6.5 %copy-start.3 = (bf16[64,1024]{1,0:T(8,128)(2,1)S(1)}, bf16[64,1024]{1,0:T(8,128)(2,1)}, u32[]{:S(2)}) copy-start(bf16[64,1024]{1,0:T(8,128)(2,1)} %param.11) | copy-start | bytes 393220
  16.6 35.0 %all-to-all-start = ((bf16[4,144,1024]{2,1,0:T(8,128)(2,1)}), bf16[4,144,1024]{2,1,0:T(8,128)(2,1)S(1)}, u32[]{:S(2)}, u32[]{:S(2)}) async-start(bf16[4,144,1024]{2,1,0:T(8,128)(2,1)} %bitcast.3), calls=%async_computation | async-start | bytes 2359296 | tf_op jit(solution)/shard_map/all_to_all | solution.py:47
  51.6 31.5 %all-to-all-start.2 = ((bf16[4,144,1024]{2,1,0:T(8,128)(2,1)}), bf16[4,144,1024]{2,1,0:T(8,128)(2,1)S(1)}, u32[]{:S(2)}, u32[]{:S(2)}) async-start(bf16[4,144,1024]{2,1,0:T(8,128)(2,1)} %fusion.10), calls=%async_computation.2 | async-start | bytes 2359296 | tf_op jit(solution)/shard_map/all_to_all | solution.py:64
  55.1 177.8 %reduce-scatter.3.cloned.1.call-start = ((), (), s32[]{:S(2)}) async-start(), calls=%async_computation.8 | async-start | bytes 10485760 | tf_op jit(solution)/shard_map/reduce_scatter | solution.py:92
  130.5 7.9 %copy-start = (bf16[4,144,1024]{2,0,1:T(4,128)(2,1)S(1)}, bf16[4,144,1024]{2,0,1:T(4,128)(2,1)}, u32[]{:S(2)}) copy-start(bf16[4,144,1024]{2,0,1:T(4,128)(2,1)} %copy.56) | copy-start | bytes 3538948
  137.3 1.1 copy-start.1
  144.2 146.3 %reduce-scatter.5.cloned.1.call-start = ((), (), s32[]{:S(2)}) async-start(), calls=%async_computation.9 | async-start | bytes 10485760 | tf_op jit(solution)/shard_map/reduce_scatter | solution.py:100
  160.0 5.8 %copy-start.2 = (bf16[4,4,36,1024]{3,2,0,1:T(8,128)(2,1)S(1)}, bf16[4,4,36,1024]{3,2,0,1:T(8,128)(2,1)}, u32[]{:S(2)}) copy-start(bf16[4,4,36,1024]{3,2,0,1:T(8,128)(2,1)} %copy-done.1) | copy-start | bytes 3538948
  161.4 33.3 %all-to-all-start.1 = ((bf16[4,144,1024]{2,1,0:T(8,128)(2,1)}), bf16[4,144,1024]{2,1,0:T(8,128)(2,1)S(1)}, u32[]{:S(2)}, u32[]{:S(2)}) async-start(bf16[4,144,1024]{2,1,0:T(8,128)(2,1)} %copy.59), calls=%async_computation.1 | async-start | bytes 2359296 | tf_op jit(solution)/shard_map/all_to_all | solution.py:63
  194.7 31.6 %all-to-all-start.3 = ((bf16[4,144,1024]{2,1,0:T(8,128)(2,1)}), bf16[4,144,1024]{2,1,0:T(8,128)(2,1)S(1)}, u32[]{:S(2)}, u32[]{:S(2)}) async-start(bf16[4,144,1024]{2,1,0:T(8,128)(2,1)} %copy.64), calls=%async_computation.3 | async-start | bytes 2359296 | tf_op jit(solution)/shard_map/all_to_all | solution.py:78
Sparse Core Ops, SparseCore 0:
  9.6 60.9 all-gather.2
  72.2 58.2 all-gather.4
  144.3 71.7 reduce-scatter.2
  218.7 71.7 reduce-scatter.4
where the time goes:
time: 307 us; the launch traced here: 306 us
  waiting for transfers between devices  181 us (59%)
  matrix products  39.6 us (13%)
  local copies, waits for them, and re-layouts  37.2 us (12%)
  starting transfers between devices  18.7 us (6%)
  other arithmetic  15.2 us (5%)
  between operations  14 us (5%)
    reduce_scatter x1, waiting for transfers between devices, local(): lax.psum_scatter(jnp.einsum('sech,secl->hel', hidden, grad_four, preferre...  48.1 us
    all_gather x1, waiting for transfers between devices, local(): lax.all_gather(down_weight, 'dp', axis=1, tiled=True)  39.9 us
    all_to_all x1, waiting for transfers between devices, local(): lax.all_to_all(send_grad, 'expert', split_axis=0, concat_axis=0, tiled=True)  25.8 us
    all_to_all x1, waiting for transfers between devices, local(): lax.all_to_all(row_grad, 'expert', split_axis=0, concat_axis=0, tiled=True)  25 us
    all_to_all x1, waiting for transfers between devices, local(): lax.all_to_all(send_rows, 'expert', split_axis=0, concat_axis=0, tiled=True)  21.5 us
    all_to_all x1, waiting for transfers between devices, local(): lax.all_to_all(result, 'expert', split_axis=0, concat_axis=0, tiled=True)  19.7 us
    unnamed x19, local copies, waits for them, and re-layouts  12.6 us
    dot_general x1, matrix products, local(): jnp.einsum('sech,secl->hel', hidden, grad_four, preferred_element_type=jn...  7.82 us
  transfers between devices with their start and end apart: 8, of which 6 were waited for; matrix products, arithmetic and copies ran while one was open for 23% of the time, Pallas kernels for 0%

commit v1 on v0

--- a/solution.py
+++ b/solution.py
@@ -2,6 +2,49 @@
 import jax.numpy as jnp
 from jax import lax
 from jax.sharding import PartitionSpec as P
+
+BOTH = ("expert", "dp")
+
+
+def by_tokens(latent_in, routes, gates, up_weight, down_weight, out_grad):
+    owners, parts = lax.axis_size("expert"), lax.axis_size("dp")
+    experts, depth, hid = up_weight.shape
+    latent = latent_in.shape[1]
+    total = experts * owners
+    width = hid // parts
+    ids = jnp.arange(total, dtype=jnp.int32)
+    chosen = routes[:, :, None] == ids[None, None, :]
+    table = jnp.sum(jnp.where(chosen, gates[:, :, None], 0.0), axis=1)
+
+    up = lax.all_to_all(up_weight, "dp", split_axis=2, concat_axis=1, tiled=True)
+    rows = lax.all_gather(latent_in, BOTH, axis=0, tiled=True)
+    dy = lax.all_gather(out_grad, BOTH, axis=0, tiled=True)
+    table_all = lax.all_gather(table, BOTH, axis=0, tiled=True)
+    first = lax.axis_index("expert") * experts
+    weight = lax.dynamic_slice_in_dim(table_all, first, experts, axis=1)
+    weight = jnp.transpose(weight)[:, :, None]
+
+    pre = jnp.einsum("tl,elh->eth", rows, up, preferred_element_type=jnp.float32)
+    back = jnp.einsum("tl,ehl->eth", dy, down_weight, preferred_element_type=jnp.float32)
+    active = jnp.where(weight > 0.0, jnp.maximum(pre, 0.0), 0.0)
+    hidden = active * active
+    gate_part = jnp.sum(hidden * back, axis=2)
+    gated = (weight * hidden).astype(jnp.bfloat16)
+    pre_grad = (weight * back * 2.0 * active).astype(jnp.bfloat16)
+    out = jnp.einsum("eth,ehl->tl", gated, down_weight, preferred_element_type=jnp.float32)
+    gin = jnp.einsum("eth,elh->tl", pre_grad, up, preferred_element_type=jnp.float32)
+    both = jnp.stack([out, gin], axis=1).astype(jnp.bfloat16)
+    both = lax.psum_scatter(both, BOTH, scatter_dimension=0, tiled=True)
+    gsum = jnp.zeros((rows.shape[0], total), jnp.float32)
+    gsum = lax.dynamic_update_slice_in_dim(gsum, jnp.transpose(gate_part), first, axis=1)
+    gsum = lax.psum_scatter(gsum, BOTH, scatter_dimension=0, tiled=True)
+    gate_grad = jnp.sum(jnp.where(chosen, gsum[:, None, :], 0.0), axis=2)
+    grad_up = jnp.einsum("tl,eth->elh", rows, pre_grad, preferred_element_type=jnp.float32)
+    grad_up = lax.all_to_all(
+        grad_up.astype(jnp.bfloat16), "dp", split_axis=1, concat_axis=2, tiled=True
+    ).astype(jnp.float32)
+    grad_down = jnp.einsum("eth,tl->ehl", gated, dy, preferred_element_type=jnp.float32)
+    return (both[:, 0], both[:, 1], gate_grad, grad_up, grad_down)
 
 
 def slot_places(routes, expert_total, capacity):
@@ -18,7 +61,7 @@
     return (places, pair_of)
 
 
-def local(latent_in, routes, gates, up_weight, down_weight, out_grad):
+def by_rows(latent_in, routes, gates, up_weight, down_weight, out_grad):
     owner_count = lax.axis_size("expert")
     local_experts = up_weight.shape[0]
     expert_total = local_experts * owner_count
@@ -110,20 +153,21 @@
     return (latent_out, grad_in, gate_grad, grad_up, grad_down)
 
 
+def local(*args):
+    token_bytes = args[0].size * 2 * lax.axis_size("expert") * lax.axis_size("dp")
+    if token_bytes <= 4 << 20:
+        return by_tokens(*args)
+    return by_rows(*args)
+
+
 def solution(mesh):
-    in_specs = (
-        P(("group", "expert", "dp"), None),
-        P(("group", "expert", "dp"), None),
-        P(("group", "expert", "dp"), None),
-        P("expert", "dp", None),
-        P("expert", "dp", None),
-        P(("group", "expert", "dp"), None),
+    tokens = P(("group", "expert", "dp"), None)
+    weights = P("expert", "dp", None)
+    grads = P(("group", "expert"), "dp", None)
+    return jax.shard_map(
+        local,
+        mesh=mesh,
+        in_specs=(tokens, tokens, tokens, weights, weights, tokens),
+        out_specs=(tokens, tokens, tokens, grads, grads),
+        check_vma=False,
     )
-    out_specs = (
-        P(("group", "expert", "dp"), None),
-        P(("group", "expert", "dp"), None),
-        P(("group", "expert", "dp"), None),
-        P(("group", "expert"), "dp", None),
-        P(("group", "expert"), "dp", None),
-    )
-    return jax.shard_map(local, mesh=mesh, in_specs=in_specs, out_specs=out_specs, check_vma=False)

time: 307 us -> 254 us (0.83)
  waiting for transfers between devices: 181 us -> 109 us
  blocking collectives: 0 us -> 48.2 us
  starting transfers between devices: 18.7 us -> 9.39 us
  matrix products: 39.6 us -> 31.1 us
  other arithmetic: 15.2 us -> 7.35 us
  local copies, waits for them, and re-layouts: 37.2 us -> 33.8 us
    all_to_all x4 -> x2, waiting for transfers between devices: 92.1 us -> 0.01 us  [the longest x1 0.01 us: by_tokens(): lax.all_to_all(up_weight, 'dp', split_axis=2, concat_axis=1, tiled=True)]
    all_gather x0 -> x1, blocking collectives: none -> 48.2 us  [by_tokens(): table_all = lax.all_gather(table, BOTH, axis=0, tiled=True)]
    unnamed x4 -> x5, waiting for transfers between devices: 1.41 us -> 30.4 us
    all_gather x2, waiting for transfers between devices: 39.9 us -> 17.1 us  [the longest x1 17.1 us: by_tokens(): dy = lax.all_gather(out_grad, BOTH, axis=0, tiled=True)]
    reduce_scatter x2 -> x1, waiting for transfers between devices: 48.1 us -> 61.6 us  [by_tokens(): both = lax.psum_scatter(both, BOTH, scatter_dimension=0, tiled=True)]
    convert_element_type x2 -> x3, local copies, waits for them, and re-layouts: 1.83 us -> 14.9 us  [the longest x2 10.6 us: by_tokens(): grad_up = lax.all_to_all(grad_up.astype(jnp.bfloat16), 'dp', split_axis=1...]
    gather x5 -> x0, local copies, waits for them, and re-layouts: 13 us -> none  [the longest x1 3.42 us: local(): send_rows = padded_in[token_of].reshape(send_shape)]
    all_to_all x4 -> x2, starting transfers between devices: 18.2 us -> 9.05 us  [the longest x1 4.58 us: by_tokens(): lax.all_to_all(up_weight, 'dp', split_axis=2, concat_axis=1, tiled=True)]
  transfers between devices with their start and end apart: 8 -> 6, of which waited for: 6 -> 3; matrix products, arithmetic and copies ran while one was open for 23% -> 21% of each run, Pallas kernels for 0% -> 0%
where the time goes in v1:
time: 254 us; the launch traced here: 253 us
  waiting for transfers between devices  109 us (43%)
  blocking collectives  48.2 us (19%)
  local copies, waits for them, and re-layouts  33.8 us (13%)
  matrix products  31.1 us (12%)
  between operations  13.9 us (5%)
  starting transfers between devices  9.39 us (4%)
  other arithmetic  7.35 us (3%)
    reduce_scatter x1, waiting for transfers between devices, by_tokens(): both = lax.psum_scatter(both, BOTH, scatter_dimension=0, tiled=True)  61.6 us
    all_gather x1, blocking collectives, by_tokens(): table_all = lax.all_gather(table, BOTH, axis=0, tiled=True)  48.2 us
    unnamed x5, waiting for transfers between devices  30.4 us
    all_gather x1, waiting for transfers between devices, by_tokens(): dy = lax.all_gather(out_grad, BOTH, axis=0, tiled=True)  17.1 us
    convert_element_type x2, local copies, waits for them, and re-layouts, by_tokens(): grad_up = lax.all_to_all(grad_up.astype(jnp.bfloat16), 'dp', split_axis=1...  10.6 us
    all_to_all x2, local copies, waits for them, and re-layouts, by_tokens(): lax.all_to_all(up_weight, 'dp', split_axis=2, concat_axis=1, tiled=True)  8.96 us
    unnamed x16, local copies, waits for them, and re-layouts  8.2 us
    dot_general x1, matrix products, by_tokens(): jnp.einsum('eth,tl->ehl', gated, dy, preferred_element_type=jnp.float32)  7.22 us
  transfers between devices with their start and end apart: 6, of which 3 were waited for; matrix products, arithmetic and copies ran while one was open for 21% of the time, Pallas kernels for 0%

profile of v1, /device:TPU:0, one launch (start us, length us, event | category | flops | bytes accessed | tf_op | source)
XLA Modules:
  0.0 252.7 jit_solution(11322861389857418956)
XLA Ops:
  8.7 4.2 %copy.48 = bf16[4,256,1024]{1,0,2:T(4,128)(2,1)} copy(bf16[4,256,1024]{2,1,0:T(8,128)(2,1)} %param.9) | data formatting | bytes 4194304 | tf_op args[3]
  12.9 4.6 %all-to-all-start = ((bf16[4,256,1024]{1,0,2:T(4,128)(2,1)}), bf16[4,256,1024]{1,0,2:T(4,128)(2,1)}, u32[]{:S(2)}, u32[]{:S(2)}) async-start(bf16[4,256,1024]{1,0,2:T(4,128)(2,1)} %copy.48), calls=%async_computation | async-start | bytes 4194304 | tf_op jit(solution)/shard_map/all_to_all | solution.py:19
  17.6 48.2 %all-gather = f32[16,64,16]{1,2,0:T(8,128)S(1)} all-gather(f32[1,64,16]{1,2,0:T(8,128)S(1)} %bitcast.78), channel_id=1, replica_groups=mesh['group'=2,'expert'=4,'dp'=4] {'expert','dp'}, dimensions={0}, use_global_device_ids=true | all-gather | bytes 69632 | tf_op jit(solution)/shard_map/all_gather | solution.py:22
  66.0 4.5 %copy.61 = bf16[4,256,4,256]{1,2,3,0:T(4,128)(2,1)} copy(bf16[4,256,4,256]{1,0,3,2:T(4,128)(2,1)} %bitcast.2) | data formatting | bytes 4194304 | tf_op jit(solution)/shard_map/all_to_all | solution.py:19
  70.5 4.4 %all_to_all.23 = bf16[4,1024,256]{1,2,0:T(8,128)(2,1)} reshape(bf16[4,4,256,256]{2,1,3,0:T(4,128)(2,1)} %bitcast.77) | data formatting | bytes 4194304 | tf_op jit(solution)/shard_map/all_to_all | solution.py:19
  74.9 4.6 %fusion.10 = f32[4,256,1024]{2,1,0:T(8,128)S(1)} fusion(bf16[4,1024,256]{1,2,0:T(8,128)(2,1)} %all_to_all.23, bf16[1024,1024]{1,0:T(8,128)(2,1)} %all-gather.4.cloned.1.call-done), kind=kOutput, calls=%fused_computation.19 | convolution fusion | flops 2147483648 | bytes 8388608 | tf_op jit(solution)/shard_map/tl,elh->eth/dot_general | solution.py:27
  79.5 2.0 copy-done.4
  81.5 3.8 %fusion.14 = bf16[1024,1,1024]{2,0,1:T(8,128)(2,1)} fusion(bf16[4,256,1024]{2,1,0:T(8,128)(2,1)S(1)} %copy-done, f32[4,256,1024]{2,1,0:T(8,128)S(1)} %fusion.10, f32[4,1024]{1,0:T(4,128)S(1)} %get-tuple-element.6, pred[4,1024]{1,0:T(4,128)(4,1)S(1)} %get-tuple-element.5), kind=kOutput, calls=%fused_computation.23 | convolution fusion | flops 2153775104 | bytes 8409088 | tf_op jit(solution)/shard_map/eth,ehl->tl/dot_general | solution.py:34
  85.3 17.1 %all-gather.6.cloned.1.call-done = bf16[1024,1024]{1,0:T(8,128)(2,1)} async-done(((bf16[64,1024]{1,0:T(8,128)(2,1)}), bf16[1024,1024]{1,0:T(8,128)(2,1)}) %all-gather.6.cloned.1.call-update) | async-done | bytes 2097168 | tf_op jit(solution)/shard_map/all_gather | solution.py:21
  102.4 5.9 %fusion.3 = (f32[4,1024]{1,0:T(4,128)S(1)}, bf16[4,1024,256]{1,2,0:T(8,128)(2,1)S(1)}) fusion(f32[4,256,1024]{2,1,0:T(8,128)} %copy-done.4, pred[4,1024]{1,0:T(4,128)(4,1)S(1)} %get-tuple-element.5, f32[4,1024]{1,0:T(4,128)S(1)} %get-tuple-element.6, bf16[4,256,1024]{2,1,0:T(8,128)(2,1)S(1)} %copy-done, bf16[1024,1024]{1,0:T(8,128)(2,1)} %all-gather.6.cloned.1.call-done), kind=kOutput, calls=%fused_computation.8 | convolution fusion | flops 2156916736 | bytes 10522624 | tf_op jit(solution)/shard_map/tl,ehl->eth/dot_general | solution.py:28
  108.3 3.8 %fusion.15 = bf16[1024,1,1024]{2,0,1:T(8,128)(2,1)} fusion(bf16[4,1024,256]{1,2,0:T(8,128)(2,1)S(1)} %get-tuple-element.8, bf16[4,1024,256]{1,2,0:T(8,128)(2,1)S(1)} %copy-done.1), kind=kOutput, calls=%fused_computation.24 | convolution fusion | flops 2148532224 | bytes 6291456 | tf_op jit(solution)/shard_map/eth,elh->tl/dot_general | solution.py:35
  112.1 1.0 copy.58
  113.4 4.6 %pad_maximum_fusion = bf16[1024,2,1024]{2,0,1:T(8,128)(2,1)} fusion(bf16[1024,1,1024]{2,0,1:T(8,128)(2,1)} %fusion.15, bf16[1024,1,1024]{2,0,1:T(8,128)(2,1)} %fusion.14), kind=kLoop, calls=%fused_computation | loop fusion | flops 2097152 | bytes 8388608 | tf_op jit(solution)/shard_map/stack | solution.py:36
  117.9 5.9 %convert_bitcast_fusion.1 = bf16[4,1024,256]{1,2,0:T(8,128)(2,1)} fusion(bf16[4,1024,256]{1,2,0:T(8,128)(2,1)} %copy-done.5, bf16[1024,1024]{1,0:T(8,128)(2,1)} %all-gather.4.cloned.1.call-done), kind=kOutput, calls=%fused_computation.22 | convolution fusion | flops 2148532224 | bytes 6291456 | tf_op jit(solution)/shard_map/tl,eth->elh/dot_general | solution.py:42
  123.9 4.3 %copy.53 = bf16[4,1024,256]{2,0,1:T(4,128)(2,1)} copy(bf16[4,1024,256]{1,2,0:T(8,128)(2,1)} %convert_bitcast_fusion.1) | data formatting | bytes 4194304 | tf_op jit(solution)/shard_map/convert_element_type | solution.py:44
  128.1 4.5 %all-to-all-start.1 = ((bf16[4,1024,256]{2,0,1:T(4,128)(2,1)}), bf16[4,1024,256]{2,0,1:T(4,128)(2,1)}, u32[]{:S(2)}, u32[]{:S(2)}) async-start(bf16[4,1024,256]{2,0,1:T(4,128)(2,1)} %copy.53), calls=%async_computation.2 | async-start | bytes 4194304 | tf_op jit(solution)/shard_map/all_to_all | solution.py:43
  132.6 7.2 %fusion.4 = f32[4,256,1024]{2,1,0:T(8,128)} fusion(bf16[1024,1024]{1,0:T(8,128)(2,1)} %all-gather.6.cloned.1.call-done, f32[4,256,1024]{2,1,0:T(8,128)} %copy-done.4, f32[4,1024]{1,0:T(4,128)S(1)} %get-tuple-element.6, pred[4,1024]{1,0:T(4,128)(4,1)S(1)} %get-tuple-element.5), kind=kOutput, calls=%fused_computation.13 | convolution fusion | flops 2152726528 | bytes 10506240 | tf_op jit(solution)/shard_map/eth,tl->ehl/dot_general | solution.py:46
  139.8 29.0 %reduce-scatter.7.cloned.1.call-done = f32[64,16]{1,0:T(8,128)} async-done(((f32[1024,16]{1,0:T(8,128)}), f32[64,16]{1,0:T(8,128)}) %reduce-scatter.7.cloned.1.call-update) | async-done | bytes 4112
  168.8 0.8 copy.59
  170.2 2.1 convert_bitcast_fusion
  172.4 4.7 %copy.54 = f32[4,256,4,256]{3,2,1,0:T(4,128)} copy(f32[4,256,4,256]{3,0,1,2:T(4,128)S(1)} %convert_bitcast_fusion) | data formatting | bytes 8388608 | tf_op jit(solution)/shard_map/convert_element_type | solution.py:45
  177.1 5.9 %reshape.20 = f32[4,256,1024]{2,1,0:T(8,128)} reshape(f32[4,256,4,256]{3,2,1,0:T(4,128)} %copy.54) | data formatting | bytes 8388608 | tf_op jit(solution)/shard_map/convert_element_type | solution.py:45
  182.9 61.6 %reduce-scatter.5.cloned.1.call-done = bf16[64,2,1024]{2,0,1:T(8,128)(2,1)} async-done(((bf16[1024,2,1024]{2,0,1:T(8,128)(2,1)}), bf16[64,2,1024]{2,0,1:T(8,128)(2,1)}) %reduce-scatter.5.cloned.1.call-update) | async-done | bytes 262160 | tf_op jit(solution)/shard_map/reduce_scatter | solution.py:37
  244.5 1.7 slice_bitcast_fusion
  (29 shorter events, 2.6 us)
Async XLA Ops:
  7.2 74.4 %copy-start = (bf16[4,256,1024]{2,1,0:T(8,128)(2,1)S(1)}, bf16[4,256,1024]{2,1,0:T(8,128)(2,1)}, u32[]{:S(2)}) copy-start(bf16[4,256,1024]{2,1,0:T(8,128)(2,1)} %param.10) | copy-start | bytes 6291460
  7.2 67.8 %all-gather.4.cloned.1.call-start = ((), (), s32[]{:S(2)}) async-start(), calls=%async_computation.4 | async-start | bytes 2228224 | tf_op jit(solution)/shard_map/all_gather | solution.py:20
  7.9 94.5 %all-gather.6.cloned.1.call-start = ((), (), s32[]{:S(2)}) async-start(), calls=%async_computation.5 | async-start | bytes 2228224 | tf_op jit(solution)/shard_map/all_gather | solution.py:21
  12.9 4.6 %copy-start.2 = (s32[64,8]{0,1:T(8,128)S(1)}, s32[64,8]{0,1:T(8,128)}, u32[]{:S(2)}) copy-start(s32[64,8]{0,1:T(8,128)} %param.7) | copy-start | bytes 6148
  12.9 4.7 %copy-start.3 = (f32[64,8]{0,1:T(8,128)S(1)}, f32[64,8]{0,1:T(8,128)}, u32[]{:S(2)}) copy-start(f32[64,8]{0,1:T(8,128)} %param.8) | copy-start | bytes 6148
  12.9 53.1 %all-to-all-start = ((bf16[4,256,1024]{1,0,2:T(4,128)(2,1)}), bf16[4,256,1024]{1,0,2:T(4,128)(2,1)}, u32[]{:S(2)}, u32[]{:S(2)}) async-start(bf16[4,256,1024]{1,0,2:T(4,128)(2,1)} %copy.48), calls=%async_computation | async-start | bytes 4194304 | tf_op jit(solution)/shard_map/all_to_all | solution.py:19
  17.5 151.3 %reduce-scatter.7.cloned.1.call-start = ((), (), s32[]{:S(2)}) async-start(), calls=%async_computation.7 | async-start | bytes 557056
  79.5 2.0 copy-start.4
  102.4 5.9 %copy-start.1 = (bf16[4,1024,256]{1,2,0:T(8,128)(2,1)S(1)}, bf16[4,1024,256]{1,2,0:T(8,128)(2,1)}, u32[]{:S(2)}) copy-start(bf16[4,1024,256]{1,2,0:T(8,128)(2,1)} %all_to_all.23) | copy-start | bytes 6291460
  108.3 3.8 %copy-start.5 = (bf16[4,1024,256]{1,2,0:T(8,128)(2,1)}, bf16[4,1024,256]{1,2,0:T(8,128)(2,1)S(1)}, u32[]{:S(2)}) copy-start(bf16[4,1024,256]{1,2,0:T(8,128)(2,1)S(1)} %get-tuple-element.8) | copy-start | bytes 6291460
  113.1 131.4 %reduce-scatter.5.cloned.1.call-start = ((), (), s32[]{:S(2)}) async-start(), calls=%async_computation.6 | async-start | bytes 4456448 | tf_op jit(solution)/shard_map/reduce_scatter | solution.py:37
  128.1 42.1 %all-to-all-start.1 = ((bf16[4,1024,256]{2,0,1:T(4,128)(2,1)}), bf16[4,1024,256]{2,0,1:T(4,128)(2,1)}, u32[]{:S(2)}, u32[]{:S(2)}) async-start(bf16[4,1024,256]{2,0,1:T(4,128)(2,1)} %copy.53), calls=%async_computation.2 | async-start | bytes 4194304 | tf_op jit(solution)/shard_map/all_to_all | solution.py:43
Sparse Core Ops, SparseCore 0:
  10.2 49.8 all-gather.3
  62.2 40.1 all-gather.5
  113.2 55.5 reduce-scatter.6
  173.0 71.4 reduce-scatter.4

commit v2 on v0

--- a/solution.py
+++ b/solution.py
@@ -1,7 +1,308 @@
+import functools
+
 import jax
 import jax.numpy as jnp
 from jax import lax
+from jax.experimental import pallas as pl
+from jax.experimental.pallas import tpu as pltpu
 from jax.sharding import PartitionSpec as P
+
+BF16, F32 = jnp.bfloat16, jnp.float32
+LANES = 128
+
+
+def dot(a, b, left=1, right=0):
+    return lax.dot_general(a, b, (((left,), (right,)), ((), ())), preferred_element_type=F32)
+
+
+def kernel(
+    owners, lat_ref, routes_ref, gates_ref, up_ref, down_ref, dy_ref,
+    out_ref, gin_ref, gate_ref, gup_ref, gdown_ref,
+    tok, tab, upt, gated, pgrad, part, gpart, prec, pgrec, xrec, xgrec, tot, gtot, zrec, zgrec,
+    gsend, grec,
+    z_s, z_r, x_s, x_r, s_s, s_r, u_s, u_r, p_s, p_r, y_s, y_r, w_s, w_r, g_s, g_r,
+):
+    block = lat_ref.shape[0]
+    experts, depth, hid = up_ref.shape
+    width = hid // 4
+    z, d = lax.axis_index("expert"), lax.axis_index("dp")
+    sib, across, diag = d + 1 - 2 * (d % 2), (d + 2) % 4, 3 - d
+    mates = (d, sib, across, diag)
+    first = z * experts
+
+    def zat(r):
+        return (z + r) % owners
+
+    def rows_of(zs):
+        return pl.ds(pl.multiple_of(zs * block, block), block)
+
+    def cut(i, size):
+        return pl.ds(pl.multiple_of(i * size, size), size)
+
+    def copy(src, dst, send, recv, where):
+        return pltpu.make_async_remote_copy(
+            src_ref=src, dst_ref=dst, send_sem=send, recv_sem=recv,
+            device_id=where, device_id_type=pl.DeviceIdType.MESH,
+        )
+
+    sent = []
+
+    def go(c):
+        c.start()
+        sent.append(c)
+
+    barrier = pltpu.get_barrier_semaphore()
+    for m in mates[1:]:
+        pl.semaphore_signal(barrier, inc=1, device_id={"dp": m}, device_id_type=pl.DeviceIdType.MESH)
+    for r in range(1, owners):
+        pl.semaphore_signal(
+            barrier, inc=1, device_id={"expert": zat(r)}, device_id_type=pl.DeviceIdType.MESH
+        )
+
+    lane = lax.broadcasted_iota(jnp.int32, (block, LANES), 1)
+    routes, gates = routes_ref[...], gates_ref[...]
+    tops = routes.shape[1]
+    table = jnp.zeros((block, LANES), F32)
+    for k in range(tops):
+        table += jnp.where(lane == routes[:, k : k + 1], gates[:, k : k + 1], 0.0)
+    tok[d, 0, rows_of(z), :] = lat_ref[...]
+    tok[d, 1, rows_of(z), :] = dy_ref[...]
+    tab[d, rows_of(z), :] = table
+    pl.semaphore_wait(barrier, 3 + owners - 1)
+
+    def blocks(dd, zs, send, recv, i, where):
+        a, b = tok.at[dd, :, rows_of(zs), :], tab.at[dd, rows_of(zs), :]
+        return (
+            copy(a, a, send.at[0, i], recv.at[0, i], where),
+            copy(b, b, send.at[1, i], recv.at[1, i], where),
+        )
+
+    def send_blocks(*args):
+        for c in blocks(*args):
+            go(c)
+
+    def wait_blocks(*args):
+        for c in blocks(*args):
+            c.wait_recv()
+
+    to_sib, to_x = {"dp": sib}, {"dp": across}
+    for r in range(1, owners):
+        send_blocks(d, z, z_s, z_r, r - 1, {"expert": zat(owners - r)})
+    send_blocks(d, z, x_s, x_r, 0, to_x)
+    send_blocks(d, z, s_s, s_r, 0, to_sib)
+    for j in (1, 2, 3):
+        m = mates[j]
+        go(copy(up_ref.at[:, :, cut(m, width)], upt.at[:, cut(d, depth), :],
+                u_s.at[j - 1], u_r.at[j - 1], {"dp": m}))
+    upt[:, cut(d, depth), :] = up_ref[:, :, cut(d, width)]
+    for r in range(1, owners):
+        wait_blocks(d, zat(r), z_s, z_r, r - 1, {"expert": zat(owners - r)})
+        send_blocks(d, zat(r), x_s, x_r, r, to_x)
+        send_blocks(d, zat(r), s_s, s_r, r, to_sib)
+
+    wide = lax.broadcasted_iota(jnp.int32, (owners * block, LANES), 1)
+
+    def inner(dd):
+        gpart[dd] = jnp.zeros((owners * block, LANES), F32)
+
+        def body(e, _):
+            pre = dot(tok[dd, 0], upt[e])
+            back = dot(tok[dd, 1], down_ref[cut(e, width), :], 1, 1)
+            here = wide == first + e
+            w = jnp.sum(jnp.where(here, tab[dd], 0.0), axis=1, keepdims=True)
+            active = jnp.where(w > 0.0, jnp.maximum(pre, 0.0), 0.0)
+            hidden = active * active
+            gpart[dd] += jnp.where(here, jnp.sum(hidden * back, axis=1, keepdims=True), 0.0)
+            gated[dd, :, cut(e, width)] = (w * hidden).astype(BF16)
+            pgrad[dd, :, cut(e, width)] = (w * back * 2.0 * active).astype(BF16)
+            return 0
+
+        lax.fori_loop(0, experts, body, 0)
+
+        def outer(n, _):
+            cols = cut(n, depth)
+            part[dd, 0, :, cols] = dot(gated[dd], down_ref[:, cols]).astype(BF16)
+            total = jnp.zeros((owners * block, depth), F32)
+            for e in range(experts):
+                total += dot(pgrad[dd, :, e * width : (e + 1) * width], upt[e, cols, :], 1, 1)
+            part[dd, 1, :, cols] = total.astype(BF16)
+            return 0
+
+        lax.fori_loop(0, 4, outer, 0)
+
+    def pair_copies(i, dd):
+        return (
+            copy(part.at[dd], prec.at[i], p_s.at[0, i], p_r.at[0, i], to_sib),
+            copy(gpart.at[dd], pgrec.at[i], p_s.at[1, i], p_r.at[1, i], to_sib),
+        )
+
+    for j in (1, 2, 3):
+        m = mates[j]
+        copy(up_ref.at[:, :, cut(m, width)], upt.at[:, cut(m, depth), :],
+             u_s.at[j - 1], u_r.at[j - 1], {"dp": m}).wait_recv()
+    for r in range(owners):
+        wait_blocks(sib, zat(r), s_s, s_r, r, to_sib)
+    inner(sib)
+    for c in pair_copies(1, sib):
+        go(c)
+    for r in range(owners):
+        wait_blocks(across, zat(r), x_s, x_r, r, to_x)
+        send_blocks(across, zat(r), s_s, s_r, owners + r, to_sib)
+    inner(d)
+    for r in range(owners):
+        wait_blocks(diag, zat(r), s_s, s_r, owners + r, to_sib)
+    inner(diag)
+    for c in pair_copies(0, diag):
+        go(c)
+    inner(across)
+    for c in pair_copies(0, diag):
+        c.wait_recv()
+
+    order = tuple(range(1, owners)) + (0,)
+
+    def cross_copies(r):
+        rows = rows_of(zat(r))
+        return (
+            copy(part.at[across, :, rows, :], xrec.at[:, rows, :], y_s.at[0, r], y_r.at[0, r], to_x),
+            copy(gpart.at[across, rows, :], xgrec.at[rows, :], y_s.at[1, r], y_r.at[1, r], to_x),
+        )
+
+    for r in order:
+        rows = rows_of(zat(r))
+        part[across, :, rows, :] = (
+            part[across, :, rows, :].astype(F32) + prec[0, :, rows, :].astype(F32)
+        ).astype(BF16)
+        gpart[across, rows, :] += pgrec[0, rows, :]
+        for c in cross_copies(r):
+            go(c)
+
+    def weight_grad(m):
+        total = jnp.zeros((depth, hid), F32)
+        for dd in range(4):
+            total += dot(tok[dd, 0, :, cut(m, depth)], pgrad[dd], 0, 0)
+        return total.astype(BF16)
+
+    def grad_copy(j):
+        return copy(gsend.at[j - 1], grec.at[j - 1], g_s.at[j - 1], g_r.at[j - 1], {"dp": mates[j]})
+
+    def spread(m, value):
+        for e in range(experts):
+            gup_ref[e, :, cut(m, width)] = value[:, e * width : (e + 1) * width]
+
+    for j in (3, 2, 1):
+        gsend[j - 1] = weight_grad(mates[j])
+        go(grad_copy(j))
+    spread(d, weight_grad(d))
+    for c in pair_copies(1, sib):
+        c.wait_recv()
+
+    def last_copies(r):
+        rows = rows_of(zat(owners - r))
+        where = {"expert": zat(owners - r)}
+        return (
+            copy(tot.at[:, rows, :], zrec.at[r - 1], w_s.at[0, r - 1], w_r.at[0, r - 1], where),
+            copy(gtot.at[rows, :], zgrec.at[r - 1], w_s.at[1, r - 1], w_r.at[1, r - 1], where),
+        )
+
+    def down_grad(e):
+        total = jnp.zeros((width, tok.shape[3]), F32)
+        for dd in range(4):
+            total += dot(gated[dd, :, e * width : (e + 1) * width], tok[dd, 1], 0, 0)
+        gdown_ref[e] = total.astype(BF16)
+
+    for i, r in enumerate(order):
+        if i < experts:
+            down_grad(i)
+        rows = rows_of(zat(r))
+        for c in cross_copies(r):
+            c.wait_recv()
+        tot[:, rows, :] = (
+            part[d, :, rows, :].astype(F32)
+            + prec[1, :, rows, :].astype(F32)
+            + xrec[:, rows, :].astype(F32)
+        ).astype(BF16)
+        gtot[rows, :] = gpart[d, rows, :] + pgrec[1, rows, :] + xgrec[rows, :]
+        if r:
+            for c in last_copies(owners - r):
+                go(c)
+    for e in range(owners, experts):
+        down_grad(e)
+    for j in (1, 3, 2):
+        grad_copy(j).wait_recv()
+        spread(mates[j], grec[j - 1])
+
+    both = tot[:, rows_of(z), :].astype(F32)
+    gsum = gtot[rows_of(z), :]
+    for r in range(1, owners):
+        for c in last_copies(r):
+            c.wait_recv()
+        both += zrec[r - 1].astype(F32)
+        gsum += zgrec[r - 1]
+    out_ref[...] = both[0].astype(BF16)
+    gin_ref[...] = both[1].astype(BF16)
+    slots = lax.broadcasted_iota(jnp.int32, (block, tops), 1)
+    found = jnp.zeros((block, tops), F32)
+    for k in range(tops):
+        mine = jnp.sum(jnp.where(lane == routes[:, k : k + 1], gsum, 0.0), axis=1, keepdims=True)
+        found += jnp.where(slots == k, mine, 0.0)
+    gate_ref[...] = found
+    for c in sent:
+        c.wait_send()
+
+
+def by_tokens(latent_in, routes, gates, up_weight, down_weight, out_grad):
+    owners = lax.axis_size("expert")
+    block, latent = latent_in.shape
+    experts, depth, hid = up_weight.shape
+    width = hid // 4
+    column = owners * block
+    vmem = pltpu.VMEM
+    dma = pltpu.SemaphoreType.DMA
+    spec = pl.BlockSpec(memory_space=pltpu.VMEM)
+    shape = jax.ShapeDtypeStruct
+    out, gin, gate, gup, gdown = pl.pallas_call(
+        functools.partial(kernel, owners),
+        out_shape=(
+            shape((block, latent), BF16),
+            shape((block, latent), BF16),
+            shape(gates.shape, F32),
+            shape((experts, depth, hid), BF16),
+            shape((experts, width, latent), BF16),
+        ),
+        in_specs=[spec] * 6,
+        out_specs=(spec,) * 5,
+        scratch_shapes=[
+            vmem((4, 2, column, latent), BF16),
+            vmem((4, column, LANES), F32),
+            vmem((experts, latent, width), BF16),
+            vmem((4, column, experts * width), BF16),
+            vmem((4, column, experts * width), BF16),
+            vmem((4, 2, column, latent), BF16),
+            vmem((4, column, LANES), F32),
+            vmem((2, 2, column, latent), BF16),
+            vmem((2, column, LANES), F32),
+            vmem((2, column, latent), BF16),
+            vmem((column, LANES), F32),
+            vmem((2, column, latent), BF16),
+            vmem((column, LANES), F32),
+            vmem((owners - 1, 2, block, latent), BF16),
+            vmem((owners - 1, block, LANES), F32),
+            vmem((3, depth, experts * width), BF16),
+            vmem((3, depth, experts * width), BF16),
+            dma((2, owners - 1)), dma((2, owners - 1)),
+            dma((2, owners)), dma((2, owners)),
+            dma((2, 2 * owners)), dma((2, 2 * owners)),
+            dma((3,)), dma((3,)),
+            dma((2, 2)), dma((2, 2)),
+            dma((2, owners)), dma((2, owners)),
+            dma((2, owners - 1)), dma((2, owners - 1)),
+            dma((3,)), dma((3,)),
+        ],
+        compiler_params=pltpu.CompilerParams(
+            collective_id=0, has_side_effects=True, vmem_limit_bytes=56 << 20
+        ),
+    )(latent_in, routes, gates, up_weight, down_weight.reshape(experts * width, latent), out_grad)
+    return out, gin, gate, gup.astype(F32), gdown.astype(F32)
 
 
 def slot_places(routes, expert_total, capacity):
@@ -18,7 +319,7 @@
     return (places, pair_of)
 
 
-def local(latent_in, routes, gates, up_weight, down_weight, out_grad):
+def by_rows(latent_in, routes, gates, up_weight, down_weight, out_grad):
     owner_count = lax.axis_size("expert")
     local_experts = up_weight.shape[0]
     expert_total = local_experts * owner_count
@@ -110,20 +411,25 @@
     return (latent_out, grad_in, gate_grad, grad_up, grad_down)
 
 
+def local(*args):
+    owners, parts = lax.axis_size("expert"), lax.axis_size("dp")
+    block, latent = args[0].shape
+    experts, depth, hid = args[3].shape
+    square = parts == 4 and hid == latent and depth * 4 == hid and hid % 512 == 0
+    small = block * owners * parts <= 1024 and latent <= 1024 and experts * owners <= LANES
+    if square and small and experts == 4 and owners > 1 and block % 16 == 0:
+        return by_tokens(*args)
+    return by_rows(*args)
+
+
 def solution(mesh):
-    in_specs = (
-        P(("group", "expert", "dp"), None),
-        P(("group", "expert", "dp"), None),
-        P(("group", "expert", "dp"), None),
-        P("expert", "dp", None),
-        P("expert", "dp", None),
-        P(("group", "expert", "dp"), None),
-    )
-    out_specs = (
-        P(("group", "expert", "dp"), None),
-        P(("group", "expert", "dp"), None),
-        P(("group", "expert", "dp"), None),
-        P(("group", "expert"), "dp", None),
-        P(("group", "expert"), "dp", None),
-    )
-    return jax.shard_map(local, mesh=mesh, in_specs=in_specs, out_specs=out_specs, check_vma=False)
+    tokens = P(("group", "expert", "dp"), None)
+    weights = P("expert", "dp", None)
+    grads = P(("group", "expert"), "dp", None)
+    return jax.shard_map(
+        local,
+        mesh=mesh,
+        in_specs=(tokens, tokens, tokens, weights, weights, tokens),
+        out_specs=(tokens, tokens, tokens, grads, grads),
+        check_vma=False,
+    )

time: 307 us -> 134 us (0.44)
  waiting for transfers between devices: 181 us -> 0 us
  Pallas kernels: 0 us -> 121 us
  matrix products: 39.6 us -> 0 us
  local copies, waits for them, and re-layouts: 37.2 us -> 5.51 us
  starting transfers between devices: 18.7 us -> 0 us
  between operations: 14 us -> 0.65 us
  other arithmetic: 15.2 us -> 6.7 us
    pallas_call x0 -> x1, Pallas kernels: none -> 121 us  [by_tokens(): pl.pallas_call(functools.partial(kernel, owners), out_shape=(shape((block...]
    all_to_all x4 -> x0, waiting for transfers between devices: 92.1 us -> none  [the longest x1 25.8 us: local(): lax.all_to_all(send_grad, 'expert', split_axis=0, concat_axis=0, tiled=True)]
    reduce_scatter x2 -> x0, waiting for transfers between devices: 48.1 us -> none  [the longest x1 48.1 us: local(): lax.psum_scatter(jnp.einsum('sech,secl->hel', hidden, grad_four, preferre...]
    all_gather x2 -> x0, waiting for transfers between devices: 39.9 us -> none  [the longest x1 39.9 us: local(): lax.all_gather(down_weight, 'dp', axis=1, tiled=True)]
    dot_general x6 -> x0, matrix products: 39.6 us -> none  [the longest x1 7.82 us: local(): jnp.einsum('sech,secl->hel', hidden, grad_four, preferred_element_type=jn...]
    all_to_all x4 -> x0, starting transfers between devices: 18.2 us -> none  [the longest x1 6.45 us: local(): lax.all_to_all(send_rows, 'expert', split_axis=0, concat_axis=0, tiled=True)]
    gather x5 -> x0, local copies, waits for them, and re-layouts: 13 us -> none  [the longest x1 3.42 us: local(): send_rows = padded_in[token_of].reshape(send_shape)]
    transpose x2 -> x0, other arithmetic: 8 us -> none  [the longest x1 4.11 us: local(): grad_up = jnp.transpose(up_sum, (1, 0, 2))]
  transfers between devices with their start and end apart: 8 -> 0, of which waited for: 6 -> 0; matrix products, arithmetic and copies ran while one was open for 23% -> 0% of each run, Pallas kernels for 0% -> 0%
where the time goes in v2:
time: 134 us
  Pallas kernels  121 us (90%)
  other arithmetic  6.7 us (5%)
  local copies, waits for them, and re-layouts  5.51 us (4%)
    pallas_call x1, Pallas kernels, by_tokens(): pl.pallas_call(functools.partial(kernel, owners), out_shape=(shape((block...  121 us
    convert_element_type x2, other arithmetic, by_tokens(): return (out, gin, gate, gup.astype(F32), gdown.astype(F32))  6.7 us
    unnamed x11, local copies, waits for them, and re-layouts  5.51 us

profile of v2, /device:TPU:0, one launch (start us, length us, event | category | flops | bytes accessed | tf_op | source)
XLA Modules:
  0.0 133.6 jit_solution(8697359436173172935)
XLA Ops:
  0.6 1.4 %copy.11.routes_ref = s32[64,8]{1,0:T(8,128)} copy(s32[64,8]{0,1:T(8,128)} %param.7) | data formatting | bytes 4096 | tf_op args[1]
  2.0 1.4 %copy.12.gates_ref = f32[64,8]{1,0:T(8,128)} copy(f32[64,8]{0,1:T(8,128)} %param.8) | data formatting | bytes 4096 | tf_op args[2]
  3.4 120.7 %shard_map.101 = (bf16[64,1024]{1,0:T(8,128)(2,1)}, bf16[64,1024]{1,0:T(8,128)(2,1)}, f32[64,8]{1,0:T(8,128)}, bf16[4,256,1024]{2,1,0:T(8,128)(2,1)}, bf16[4,256,1024]{2,1,0:T(8,128)(2,1)}) custom-call(bf16[64,1024]{1,0:T(8,128)(2,1)} %lat_ref.1, s32[64,8]{1,0:T(8,128)} %copy.11.routes_ref, f32[64,8]{1,0:T(8,128)} %copy.12.gates_ref, ...), custom_call_target="tpu_custom_call" | custom-call | tf_op jit(solution)/shard_map/pallas_call | solution.py:263
  124.1 1.4 %copy.13 = f32[64,8]{0,1:T(8,128)} copy(f32[64,8]{1,0:T(8,128)} %get-tuple-element.17) | data formatting | bytes 4096
  125.6 0.0 copy-start
  125.6 4.2 %convert_element_type.6 = f32[4,256,1024]{2,1,0:T(8,128)} convert(bf16[4,256,1024]{2,1,0:T(8,128)(2,1)} %get-tuple-element.13) | non-fusion elementwise | flops 1048576 | bytes 6291456 | tf_op jit(solution)/shard_map/convert_element_type | solution.py:305
  129.8 0.0 copy-done
  129.8 0.0 copy-start.2
  129.8 0.0 copy-start.1
  129.8 2.5 %convert_element_type.7 = f32[4,256,1024]{2,1,0:T(8,128)} convert(bf16[4,256,1024]{2,1,0:T(8,128)(2,1)S(1)} %copy-done) | non-fusion elementwise | flops 1048576 | bytes 6291456 | tf_op jit(solution)/shard_map/convert_element_type | solution.py:305
  132.3 0.0 copy-done.2
  132.3 0.7 copy.16
  132.9 0.0 copy-done.1
  132.9 0.7 copy.17
Async XLA Ops:
  125.6 4.2 %copy-start = (bf16[4,256,1024]{2,1,0:T(8,128)(2,1)S(1)}, bf16[4,256,1024]{2,1,0:T(8,128)(2,1)}, u32[]{:S(2)}) copy-start(bf16[4,256,1024]{2,1,0:T(8,128)(2,1)} %get-tuple-element.14) | copy-start | bytes 6291460
  129.8 2.5 %copy-start.2 = (bf16[64,1024]{1,0:T(8,128)(2,1)S(1)}, bf16[64,1024]{1,0:T(8,128)(2,1)}, u32[]{:S(2)}) copy-start(bf16[64,1024]{1,0:T(8,128)(2,1)} %get-tuple-element.25) | copy-start | bytes 393220
  129.8 3.1 %copy-start.1 = (bf16[64,1024]{1,0:T(8,128)(2,1)S(1)}, bf16[64,1024]{1,0:T(8,128)(2,1)}, u32[]{:S(2)}) copy-start(bf16[64,1024]{1,0:T(8,128)(2,1)} %get-tuple-element.26) | copy-start | bytes 393220

commit v3 on v2

--- a/solution.py
+++ b/solution.py
@@ -20,12 +20,16 @@
     out_ref, gin_ref, gate_ref, gup_ref, gdown_ref,
     tok, tab, upt, gated, pgrad, part, gpart, prec, pgrec, xrec, xgrec, tot, gtot, zrec, zgrec,
     gsend, grec,
-    z_s, z_r, x_s, x_r, s_s, s_r, u_s, u_r, p_s, p_r, y_s, y_r, w_s, w_r, g_s, g_r,
+    z_s, z_r, x_s, x_r, s_s, s_r, u_s, u_r, v_s, v_r, p_s, p_r, y_s, y_r, w_s, w_r, g_s, g_r,
 ):
     block = lat_ref.shape[0]
     experts, depth, hid = up_ref.shape
     width = hid // 4
     z, d = lax.axis_index("expert"), lax.axis_index("dp")
+    group = lax.axis_index("group")
+    half = experts // 2
+    my_half, other_half = pl.ds(group * half, half), pl.ds((1 - group) * half, half)
+    to_twin = {"group": 1 - group}
     sib, across, diag = d + 1 - 2 * (d % 2), (d + 2) % 4, 3 - d
     mates = (d, sib, across, diag)
     first = z * experts
@@ -59,8 +63,10 @@
             barrier, inc=1, device_id={"expert": zat(r)}, device_id_type=pl.DeviceIdType.MESH
         )
 
+    pl.semaphore_signal(barrier, inc=1, device_id=to_twin, device_id_type=pl.DeviceIdType.MESH)
+
     lane = lax.broadcasted_iota(jnp.int32, (block, LANES), 1)
-    routes, gates = routes_ref[...], gates_ref[...]
+    routes, gates = jnp.transpose(routes_ref[...]), jnp.transpose(gates_ref[...])
     tops = routes.shape[1]
     table = jnp.zeros((block, LANES), F32)
     for k in range(tops):
@@ -68,7 +74,7 @@
     tok[d, 0, rows_of(z), :] = lat_ref[...]
     tok[d, 1, rows_of(z), :] = dy_ref[...]
     tab[d, rows_of(z), :] = table
-    pl.semaphore_wait(barrier, 3 + owners - 1)
+    pl.semaphore_wait(barrier, 3 + owners - 1 + 1)
 
     def blocks(dd, zs, send, recv, i, where):
         a, b = tok.at[dd, :, rows_of(zs), :], tab.at[dd, rows_of(zs), :]
@@ -90,19 +96,32 @@
         send_blocks(d, z, z_s, z_r, r - 1, {"expert": zat(owners - r)})
     send_blocks(d, z, x_s, x_r, 0, to_x)
     send_blocks(d, z, s_s, s_r, 0, to_sib)
-    for j in (1, 2, 3):
+
+    def up_copy(j, source, target):
         m = mates[j]
-        go(copy(up_ref.at[:, :, cut(m, width)], upt.at[:, cut(d, depth), :],
-                u_s.at[j - 1], u_r.at[j - 1], {"dp": m}))
+        es = slice(None) if j == 1 else my_half
+        return copy(up_ref.at[es, :, cut(target, width)], upt.at[es, cut(source, depth), :],
+                    u_s.at[j - 1], u_r.at[j - 1], {"dp": m})
+
+    def twin_copy(j, es):
+        part_of = upt.at[es, cut(mates[j], depth), :]
+        return copy(part_of, part_of, v_s.at[j - 2], v_r.at[j - 2], to_twin)
+
+    for j in (2, 3, 1):
+        go(up_copy(j, d, mates[j]))
     upt[:, cut(d, depth), :] = up_ref[:, :, cut(d, width)]
     for r in range(1, owners):
         wait_blocks(d, zat(r), z_s, z_r, r - 1, {"expert": zat(owners - r)})
         send_blocks(d, zat(r), x_s, x_r, r, to_x)
         send_blocks(d, zat(r), s_s, s_r, r, to_sib)
+        if r == min(2, owners - 1):
+            for j in (2, 3):
+                up_copy(j, mates[j], d).wait_recv()
+                go(twin_copy(j, my_half))
 
     wide = lax.broadcasted_iota(jnp.int32, (owners * block, LANES), 1)
 
-    def inner(dd):
+    def activate(dd):
         gpart[dd] = jnp.zeros((owners * block, LANES), F32)
 
         def body(e, _):
@@ -119,6 +138,7 @@
 
         lax.fori_loop(0, experts, body, 0)
 
+    def project(dd):
         def outer(n, _):
             cols = cut(n, depth)
             part[dd, 0, :, cols] = dot(gated[dd], down_ref[:, cols]).astype(BF16)
@@ -136,25 +156,25 @@
             copy(gpart.at[dd], pgrec.at[i], p_s.at[1, i], p_r.at[1, i], to_sib),
         )
 
-    for j in (1, 2, 3):
-        m = mates[j]
-        copy(up_ref.at[:, :, cut(m, width)], upt.at[:, cut(m, depth), :],
-             u_s.at[j - 1], u_r.at[j - 1], {"dp": m}).wait_recv()
-    for r in range(owners):
-        wait_blocks(sib, zat(r), s_s, s_r, r, to_sib)
-    inner(sib)
-    for c in pair_copies(1, sib):
-        go(c)
+    up_copy(1, sib, d).wait_recv()
+    for j in (2, 3):
+        twin_copy(j, other_half).wait_recv()
+    activate(d)
+    project(d)
     for r in range(owners):
         wait_blocks(across, zat(r), x_s, x_r, r, to_x)
         send_blocks(across, zat(r), s_s, s_r, owners + r, to_sib)
-    inner(d)
+    activate(across)
     for r in range(owners):
         wait_blocks(diag, zat(r), s_s, s_r, owners + r, to_sib)
-    inner(diag)
+    activate(diag)
+    project(diag)
     for c in pair_copies(0, diag):
         go(c)
-    inner(across)
+    project(across)
+    for r in range(owners):
+        wait_blocks(sib, zat(r), s_s, s_r, r, to_sib)
+    activate(sib)
     for c in pair_copies(0, diag):
         c.wait_recv()
 
@@ -189,9 +209,12 @@
         for e in range(experts):
             gup_ref[e, :, cut(m, width)] = value[:, e * width : (e + 1) * width]
 
+    project(sib)
+    for c in pair_copies(1, sib):
+        go(c)
     for j in (3, 2, 1):
         gsend[j - 1] = weight_grad(mates[j])
-        go(grad_copy(j))
+    go(grad_copy(1))
     spread(d, weight_grad(d))
     for c in pair_copies(1, sib):
         c.wait_recv()
@@ -216,6 +239,10 @@
         rows = rows_of(zat(r))
         for c in cross_copies(r):
             c.wait_recv()
+        if i == min(1, owners - 1):
+            go(grad_copy(3))
+        if i == min(2, owners - 1):
+            go(grad_copy(2))
         tot[:, rows, :] = (
             part[d, :, rows, :].astype(F32)
             + prec[1, :, rows, :].astype(F32)
@@ -227,9 +254,8 @@
                 go(c)
     for e in range(owners, experts):
         down_grad(e)
-    for j in (1, 3, 2):
-        grad_copy(j).wait_recv()
-        spread(mates[j], grec[j - 1])
+    grad_copy(1).wait_recv()
+    spread(sib, grec[0])
 
     both = tot[:, rows_of(z), :].astype(F32)
     gsum = gtot[rows_of(z), :]
@@ -245,7 +271,10 @@
     for k in range(tops):
         mine = jnp.sum(jnp.where(lane == routes[:, k : k + 1], gsum, 0.0), axis=1, keepdims=True)
         found += jnp.where(slots == k, mine, 0.0)
-    gate_ref[...] = found
+    gate_ref[...] = jnp.transpose(found)
+    for j in (3, 2):
+        grad_copy(j).wait_recv()
+        spread(mates[j], grec[j - 1])
     for c in sent:
         c.wait_send()
 
@@ -265,7 +294,7 @@
         out_shape=(
             shape((block, latent), BF16),
             shape((block, latent), BF16),
-            shape(gates.shape, F32),
+            shape(gates.shape[::-1], F32),
             shape((experts, depth, hid), BF16),
             shape((experts, width, latent), BF16),
         ),
@@ -293,6 +322,7 @@
             dma((2, owners)), dma((2, owners)),
             dma((2, 2 * owners)), dma((2, 2 * owners)),
             dma((3,)), dma((3,)),
+            dma((2,)), dma((2,)),
             dma((2, 2)), dma((2, 2)),
             dma((2, owners)), dma((2, owners)),
             dma((2, owners - 1)), dma((2, owners - 1)),
@@ -301,8 +331,11 @@
         compiler_params=pltpu.CompilerParams(
             collective_id=0, has_side_effects=True, vmem_limit_bytes=56 << 20
         ),
-    )(latent_in, routes, gates, up_weight, down_weight.reshape(experts * width, latent), out_grad)
-    return out, gin, gate, gup.astype(F32), gdown.astype(F32)
+    )(
+        latent_in, routes.T, gates.T, up_weight,
+        down_weight.reshape(experts * width, latent), out_grad,
+    )
+    return out, gin, gate.T, gup.astype(F32), gdown.astype(F32)
 
 
 def slot_places(routes, expert_total, capacity):
@@ -415,7 +448,7 @@
     owners, parts = lax.axis_size("expert"), lax.axis_size("dp")
     block, latent = args[0].shape
     experts, depth, hid = args[3].shape
-    square = parts == 4 and hid == latent and depth * 4 == hid and hid % 512 == 0
+    square = parts == 4 and lax.axis_size("group") == 2 and hid == latent and depth * 4 == hid and hid % 512 == 0
     small = block * owners * parts <= 1024 and latent <= 1024 and experts * owners <= LANES
     if square and small and experts == 4 and owners > 1 and block % 16 == 0:
         return by_tokens(*args)

time: 134 us -> 124 us (0.925)
  Pallas kernels: 121 us -> 114 us
  local copies, waits for them, and re-layouts: 5.51 us -> 1.92 us
    pallas_call x1, Pallas kernels: 121 us -> 114 us  [by_tokens(): pl.pallas_call(functools.partial(kernel, owners), out_shape=(shape((block...]
    unnamed x11, local copies, waits for them, and re-layouts: 5.51 us -> 1.92 us
where the time goes in v3:
time: 124 us
  Pallas kernels  114 us (92%)
  other arithmetic  6.7 us (5%)
  local copies, waits for them, and re-layouts  1.92 us (2%)
    pallas_call x1, Pallas kernels, by_tokens(): pl.pallas_call(functools.partial(kernel, owners), out_shape=(shape((block...  114 us
    convert_element_type x2, other arithmetic, by_tokens(): return (out, gin, gate.T, gup.astype(F32), gdown.astype(F32))  6.7 us

profile of v3, /device:TPU:0, one launch (start us, length us, event | category | flops | bytes accessed | tf_op | source)
XLA Modules:
  0.0 123.7 jit_solution(16412778726655538109)
XLA Ops:
  0.6 114.4 %shard_map.101 = (bf16[64,1024]{1,0:T(8,128)(2,1)}, bf16[64,1024]{1,0:T(8,128)(2,1)}, f32[8,64]{1,0:T(8,128)}, bf16[4,256,1024]{2,1,0:T(8,128)(2,1)}, bf16[4,256,1024]{2,1,0:T(8,128)(2,1)}) custom-call(bf16[64,1024]{1,0:T(8,128)(2,1)} %lat_ref.1, s32[8,64]{1,0:T(8,128)} %bitcast.6, f32[8,64]{1,0:T(8,128)} %bitcast.7, bf16[4,256,1024]{2,1,0:T(8,128)(2,1)} %up_ref.1, ...), custom_call_target="tpu_custom_call" | custom-call | tf_op jit(solution)/shard_map/pallas_call | solution.py:292
  115.0 0.0 copy-start
  115.0 4.2 %convert_element_type.6 = f32[4,256,1024]{2,1,0:T(8,128)} convert(bf16[4,256,1024]{2,1,0:T(8,128)(2,1)} %get-tuple-element.13) | non-fusion elementwise | flops 1048576 | bytes 6291456 | tf_op jit(solution)/shard_map/convert_element_type | solution.py:338
  119.2 0.0 copy-done
  119.3 0.0 copy-start.2
  119.3 0.0 copy-start.1
  119.3 0.0 copy-start.3
  119.3 2.5 %convert_element_type.7 = f32[4,256,1024]{2,1,0:T(8,128)} convert(bf16[4,256,1024]{2,1,0:T(8,128)(2,1)S(1)} %copy-done) | non-fusion elementwise | flops 1048576 | bytes 6291456 | tf_op jit(solution)/shard_map/convert_element_type | solution.py:338
  121.7 0.0 copy-done.2
  121.7 0.7 copy.14
  122.4 0.0 copy-done.1
  122.4 0.7 copy.15
  123.1 0.0 copy-done.3
  123.1 0.6 copy.16
Async XLA Ops:
  115.0 4.2 %copy-start = (bf16[4,256,1024]{2,1,0:T(8,128)(2,1)S(1)}, bf16[4,256,1024]{2,1,0:T(8,128)(2,1)}, u32[]{:S(2)}) copy-start(bf16[4,256,1024]{2,1,0:T(8,128)(2,1)} %get-tuple-element.14) | copy-start | bytes 6291460
  119.3 2.5 %copy-start.2 = (bf16[64,1024]{1,0:T(8,128)(2,1)S(1)}, bf16[64,1024]{1,0:T(8,128)(2,1)}, u32[]{:S(2)}) copy-start(bf16[64,1024]{1,0:T(8,128)(2,1)} %get-tuple-element.20) | copy-start | bytes 393220
  119.3 3.2 %copy-start.1 = (bf16[64,1024]{1,0:T(8,128)(2,1)S(1)}, bf16[64,1024]{1,0:T(8,128)(2,1)}, u32[]{:S(2)}) copy-start(bf16[64,1024]{1,0:T(8,128)(2,1)} %get-tuple-element.21) | copy-start | bytes 393220
  119.3 3.8 %copy-start.3 = (f32[8,64]{1,0:T(8,128)S(1)}, f32[8,64]{1,0:T(8,128)}, u32[]{:S(2)}) copy-start(f32[8,64]{1,0:T(8,128)} %get-tuple-element.12) | copy-start | bytes 6148

commit v4 on v3

--- a/solution.py
+++ b/solution.py
@@ -172,9 +172,6 @@
     for c in pair_copies(0, diag):
         go(c)
     project(across)
-    for r in range(owners):
-        wait_blocks(sib, zat(r), s_s, s_r, r, to_sib)
-    activate(sib)
     for c in pair_copies(0, diag):
         c.wait_recv()
 
@@ -209,6 +206,9 @@
         for e in range(experts):
             gup_ref[e, :, cut(m, width)] = value[:, e * width : (e + 1) * width]
 
+    for r in range(owners):
+        wait_blocks(sib, zat(r), s_s, s_r, r, to_sib)
+    activate(sib)
     project(sib)
     for c in pair_copies(1, sib):
         go(c)

time: 124 us -> 122 us (0.984)
    pallas_call x1, Pallas kernels: 114 us -> 113 us  [by_tokens(): pl.pallas_call(functools.partial(kernel, owners), out_shape=(shape((block...]
where the time goes in v4:
time: 122 us
  Pallas kernels  113 us (93%)
  other arithmetic  6.7 us (5%)
  local copies, waits for them, and re-layouts  1.92 us (2%)
    pallas_call x1, Pallas kernels, by_tokens(): pl.pallas_call(functools.partial(kernel, owners), out_shape=(shape((block...  113 us
    convert_element_type x2, other arithmetic, by_tokens(): return (out, gin, gate.T, gup.astype(F32), gdown.astype(F32))  6.7 us

profile of v4, /device:TPU:0, one launch (start us, length us, event | category | flops | bytes accessed | tf_op | source)
XLA Modules:
  0.0 121.9 jit_solution(3796274705871862870)
XLA Ops:
  0.6 112.7 %shard_map.101 = (bf16[64,1024]{1,0:T(8,128)(2,1)}, bf16[64,1024]{1,0:T(8,128)(2,1)}, f32[8,64]{1,0:T(8,128)}, bf16[4,256,1024]{2,1,0:T(8,128)(2,1)}, bf16[4,256,1024]{2,1,0:T(8,128)(2,1)}) custom-call(bf16[64,1024]{1,0:T(8,128)(2,1)} %lat_ref.1, s32[8,64]{1,0:T(8,128)} %bitcast.6, f32[8,64]{1,0:T(8,128)} %bitcast.7, bf16[4,256,1024]{2,1,0:T(8,128)(2,1)} %up_ref.1, ...), custom_call_target="tpu_custom_call" | custom-call | tf_op jit(solution)/shard_map/pallas_call | solution.py:292
  113.3 0.0 copy-start
  113.3 4.2 %convert_element_type.6 = f32[4,256,1024]{2,1,0:T(8,128)} convert(bf16[4,256,1024]{2,1,0:T(8,128)(2,1)} %get-tuple-element.13) | non-fusion elementwise | flops 1048576 | bytes 6291456 | tf_op jit(solution)/shard_map/convert_element_type | solution.py:338
  117.5 0.0 copy-done
  117.5 0.0 copy-start.2
  117.5 0.0 copy-start.1
  117.5 0.0 copy-start.3
  117.5 2.5 %convert_element_type.7 = f32[4,256,1024]{2,1,0:T(8,128)} convert(bf16[4,256,1024]{2,1,0:T(8,128)(2,1)S(1)} %copy-done) | non-fusion elementwise | flops 1048576 | bytes 6291456 | tf_op jit(solution)/shard_map/convert_element_type | solution.py:338
  120.0 0.0 copy-done.2
  120.0 0.7 copy.14
  120.7 0.0 copy-done.1
  120.7 0.7 copy.15
  121.3 0.0 copy-done.3
  121.4 0.6 copy.16
Async XLA Ops:
  113.3 4.2 %copy-start = (bf16[4,256,1024]{2,1,0:T(8,128)(2,1)S(1)}, bf16[4,256,1024]{2,1,0:T(8,128)(2,1)}, u32[]{:S(2)}) copy-start(bf16[4,256,1024]{2,1,0:T(8,128)(2,1)} %get-tuple-element.14) | copy-start | bytes 6291460
  117.5 2.5 %copy-start.2 = (bf16[64,1024]{1,0:T(8,128)(2,1)S(1)}, bf16[64,1024]{1,0:T(8,128)(2,1)}, u32[]{:S(2)}) copy-start(bf16[64,1024]{1,0:T(8,128)(2,1)} %get-tuple-element.20) | copy-start | bytes 393220
  117.5 3.2 %copy-start.1 = (bf16[64,1024]{1,0:T(8,128)(2,1)S(1)}, bf16[64,1024]{1,0:T(8,128)(2,1)}, u32[]{:S(2)}) copy-start(bf16[64,1024]{1,0:T(8,128)(2,1)} %get-tuple-element.21) | copy-start | bytes 393220
  117.5 3.8 %copy-start.3 = (f32[8,64]{1,0:T(8,128)S(1)}, f32[8,64]{1,0:T(8,128)}, u32[]{:S(2)}) copy-start(f32[8,64]{1,0:T(8,128)} %get-tuple-element.12) | copy-start | bytes 6148
